TPU v7x, 256 devices: a whole 4x4x8 slice. The times are simulated.
256 devices in a mesh: rows: 32 (over z_hi, y, x), cols: 8 (over z_lo, core).
Axes of the slice: x: 4, y: 4, z: 8 (z_hi: 2, z_lo: 4; z = z_hi * 4 + z_lo), core: 2. Of those that a mesh axis runs over, the one named last changes fastest.
Arguments:
- logged: bfloat16 [32768, 256], P(('rows', 'cols')), may hold values from -8 to 8
- fresh: bfloat16 [65536, 256], P(('cols', 'rows')), may hold values from -6 to 6
- warm: float32 [65536], P('cols'), may hold values from -1 to 1
Outputs:
- row_potential: float32 [32768], P('rows')
- col_potential: float32 [65536], P('cols')
- reward: float32 [32768], P('rows')
All inputs are finite; a program needn't handle non-finite values.
Results may differ from a plain program's by a relative error of at most 0.0013.
Values may be sent and summed in bfloat16 or wider, within the bound.
No kernel may reach another device: no remote copies, remote signals or barrier semaphores. Data moves between devices by JAX's collectives and lax.ppermute only.
A program may use at most 128 MiB of HBM per device.

v0:
```python
import functools
import math

import jax
import jax.numpy as jnp
from jax import lax
from jax.experimental import pallas as pl
from jax.experimental.pallas import tpu as pltpu
from jax.sharding import Mesh
from jax.sharding import PartitionSpec as P

EPS = 0.01
AXES = ("zh", "y", "x", "zl", "core")
ROW_GROUP = ("zh", "zl", "core")
COL_GROUP = ("y", "x")
LN2 = math.log(2.0)
LOG2E = 1.0 / LN2


def nt_dot(a, b):
    return lax.dot_general(a, b, (((1,), (1,)), ((), ())), preferred_element_type=jnp.float32)


SAMPLE = 16
LARGEST, SMALLEST = 2.0**110, 2.0**-100


def to_row(column, copies=1):
    row = jnp.broadcast_to(column, (column.shape[0], 128)).T[:1]
    return jnp.broadcast_to(row[None], (copies,) + row.shape)


def lse_kernel(scale, blocks, raised, x_ref, y_ref, bias_ref, few_ref, out_ref, moved_ref):
    rows, cols = x_ref.shape[0], y_ref.shape[0]
    copies = out_ref.shape[0]
    step = rows // 16
    some = jnp.concatenate([x_ref[s : s + 2 * SAMPLE, :] for s in range(0, rows, step)], axis=0)
    step = cols // 16
    few = jnp.concatenate([y_ref[s : s + SAMPLE, :] for s in range(0, cols, step)], axis=0)
    seen = nt_dot(some, few) * scale + few_ref[...]
    seen = jnp.maximum(seen[:, :128], seen[:, 128:]).reshape(blocks, -1, 128)
    offset = jnp.max(jnp.max(seen, axis=1), axis=1, keepdims=True) - raised
    moved_ref[...] = bias_ref[...] - offset

    size = rows // blocks
    totals = [jnp.zeros((size, 128), jnp.float32)] * blocks
    for start in range(0, cols, 256):
        prod = nt_dot(x_ref[...], y_ref[start : start + 256, :])
        for b in range(blocks):
            for o in (0, 128):
                part = prod[b * size : (b + 1) * size, o : o + 128]
                at = slice(start + o, start + o + 128)
                totals[b] = totals[b] + jnp.exp2(part * scale + moved_ref[b : b + 1, at])
    safe = None
    for b in range(blocks):
        total = jnp.sum(totals[b], axis=1, keepdims=True)
        value = jnp.log2(total) + offset[b : b + 1, :]
        out_ref[:, :, b * size : (b + 1) * size] = to_row(value, copies)
        good = jnp.logical_and(jnp.min(total) > SMALLEST, jnp.max(total) < LARGEST)
        safe = good if safe is None else jnp.logical_and(safe, good)

    @pl.when(jnp.logical_not(safe))
    def _():
        def some_rows(r, _):
            own = pl.ds(pl.multiple_of(r * 128, 128), 128)
            xs = x_ref[own, :]

            def some_columns(c, state):
                top, total = state
                at = pl.ds(pl.multiple_of(c * 128, 128), 128)
                part = nt_dot(xs, y_ref[at, :]) * scale + bias_ref[:, at]
                new = jnp.maximum(top, part)
                return new, total * jnp.exp2(top - new) + jnp.exp2(part - new)

            state = jnp.full((128, 128), -1e38, jnp.float32), jnp.zeros((128, 128), jnp.float32)
            top, total = lax.fori_loop(0, cols // 128, some_columns, state)
            best = jnp.max(top, axis=1, keepdims=True)
            total = jnp.sum(total * jnp.exp2(top - best), axis=1, keepdims=True)
            out_ref[:, :, own] = to_row(best + jnp.log2(total), copies)
            return 0

        lax.fori_loop(0, rows // 128, some_rows, 0)


def lse(x, y, bias, scale, blocks, raised, copies=16):
    rows, depth = x.shape
    cols = y.shape[0]
    few = bias.reshape(16, cols // 16)[:, :SAMPLE].reshape(1, 16 * SAMPLE)
    return pl.pallas_call(
        functools.partial(lse_kernel, scale, blocks, raised),
        out_shape=jax.ShapeDtypeStruct((copies, 1, rows), jnp.float32),
        scratch_shapes=[pltpu.VMEM((blocks, cols), jnp.float32)],
        compiler_params=pltpu.CompilerParams(vmem_limit_bytes=40 * 2**20),
        cost_estimate=pl.CostEstimate(
            flops=2 * rows * cols * depth, bytes_accessed=2 * depth * (rows + cols), transcendentals=rows * cols
        ),
    )(x, y, bias.reshape(1, cols), few)


def over_lanes(row):
    high = row.astype(jnp.bfloat16)
    rest = row - high.astype(jnp.float32)
    mid = rest.astype(jnp.bfloat16)
    low = (rest - mid.astype(jnp.float32)).astype(jnp.bfloat16)
    parts = jnp.concatenate([high, mid, low, jnp.zeros((13, row.shape[1]), jnp.bfloat16)], axis=0)
    ones = jnp.ones((16, 128), jnp.bfloat16)
    return lax.dot_general(parts, ones, (((0,), (0,)), ((), ())), preferred_element_type=jnp.float32)


def fold(a, height):
    return jnp.sum(a.reshape(a.shape[0] // height, height, a.shape[1]), axis=0)


MB = 512
HEADROOM = 40.0
HEADROOM_LIMIT = -160.0


def column_kernel(scale, raised, x_ref, y_ref, rbias_ref, rsq_ref, csq_ref, out_ref, low_ref, high_ref, info_ref, wide_ref, pot_ref):
    rows, cols = x_ref.shape[0], y_ref.shape[0]
    copies = out_ref.shape[0]
    wide_ref[...] = over_lanes(rbias_ref[...])
    step = cols // 16
    some = jnp.concatenate([y_ref[s : s + 2 * SAMPLE, :] for s in range(0, cols, step)], axis=0)
    step = rows // 16
    few = jnp.concatenate([x_ref[s : s + SAMPLE, :] for s in range(0, rows, step)], axis=0)
    few_bias = jnp.concatenate([wide_ref[s : s + SAMPLE, :] for s in range(0, rows, step)], axis=0)
    seen = nt_dot(few, some)
    seen = functools.reduce(jnp.maximum, [seen[:, o : o + 128] * scale + few_bias for o in range(0, 512, 128)])
    offset = jnp.max(jnp.max(seen, axis=0, keepdims=True), axis=1, keepdims=True) - raised
    wide_ref[...] = wide_ref[...] - offset
    pot_ref[...] = over_lanes(rbias_ref[...] + (0.5 * scale) * rsq_ref[...] - offset)

    smallest = largest = None
    for t in range(0, cols, 256):
        totals = [jnp.zeros((32, 128), jnp.float32)] * 2
        for start in range(0, rows, MB):
            prod = nt_dot(x_ref[start : start + MB, :], y_ref[t : t + 256, :])
            wide = wide_ref[start : start + MB, :]
            pot = pot_ref[start : start + MB, :]
            for b in (0, 1):
                at = slice(t + b * 128, t + b * 128 + 128)
                power = prod[:, b * 128 : b * 128 + 128] * scale + wide
                term = jnp.exp2(power)
                totals[b] = totals[b] + fold(term, 32)
                terms_ref = low_ref if start < rows // 2 else high_ref
                place = start % (rows // 2)
                terms_ref[place : place + MB, at] = term * ((scale * csq_ref[:, at] - power) + pot)
        for b in (0, 1):
            total = jnp.sum(totals[b], axis=0, keepdims=True)
            smallest = total if smallest is None else jnp.minimum(smallest, total)
            largest = total if largest is None else jnp.maximum(largest, total)
            at = slice(t + b * 128, t + b * 128 + 128)
            out_ref[:, :, at] = jnp.broadcast_to((jnp.log2(total) + offset)[None], (copies, 1, 128))
    safe = jnp.logical_and(jnp.min(smallest) > SMALLEST, jnp.max(largest) < LARGEST)
    info_ref[:1, :] = jnp.broadcast_to(offset, (1, 128))
    info_ref[1:, :] = jnp.broadcast_to(jnp.where(safe, 1.0, 0.0), (1, 128))

    @pl.when(jnp.logical_not(safe))
    def _():
        def some_columns(c, _):
            own = pl.ds(pl.multiple_of(c * 128, 128), 128)
            ys = y_ref[own, :]

            def some_rows(r, state):
                top, total = state
                at = pl.ds(pl.multiple_of(r * 128, 128), 128)
                part = nt_dot(ys, x_ref[at, :]) * scale + rbias_ref[:, at]
                new = jnp.maximum(top, part)
                return new, total * jnp.exp2(top - new) + jnp.exp2(part - new)

            state = jnp.full((128, 128), -1e38, jnp.float32), jnp.zeros((128, 128), jnp.float32)
            top, total = lax.fori_loop(0, rows // 128, some_rows, state)
            best = jnp.max(top, axis=1, keepdims=True)
            total = jnp.sum(total * jnp.exp2(top - best), axis=1, keepdims=True)
            out_ref[:, :, own] = to_row(best + jnp.log2(total), copies)
            return 0

        lax.fori_loop(0, cols // 128, some_columns, 0)


def column_part(x, y, rbias, rsq, csq, scale, raised, copies=16):
    rows, depth = x.shape
    cols = y.shape[0]
    vmem = pl.BlockSpec(memory_space=pltpu.VMEM)
    return pl.pallas_call(
        functools.partial(column_kernel, scale, raised),
        in_specs=[vmem] * 5,
        out_specs=[vmem] * 4,
        out_shape=[
            jax.ShapeDtypeStruct((copies, 1, cols), jnp.float32),
            jax.ShapeDtypeStruct((rows // 2, cols), jnp.float32),
            jax.ShapeDtypeStruct((rows // 2, cols), jnp.float32),
            jax.ShapeDtypeStruct((2, 128), jnp.float32),
        ],
        scratch_shapes=[pltpu.VMEM((rows, 128), jnp.float32)] * 2,
        compiler_params=pltpu.CompilerParams(vmem_limit_bytes=8 * 2**20),
        cost_estimate=pl.CostEstimate(
            flops=2 * rows * cols * depth, bytes_accessed=2 * depth * (rows + cols), transcendentals=rows * cols
        ),
    )(x, y, rbias, rsq, csq)


def reward_kernel(
    scale, factor, n_cols, parts_ref, x_ref, y_ref, rbias_ref, rsq_ref, csq_ref, low_ref, high_ref, info_ref, out_ref, pot_ref, cbias_ref
):
    rows, cols = x_ref.shape[0], y_ref.shape[0]
    half = rows // 2
    best = functools.reduce(jnp.maximum, [parts_ref[i] for i in range(parts_ref.shape[0])])
    total = functools.reduce(jnp.add, [jnp.exp2(parts_ref[i] - best) for i in range(parts_ref.shape[0])])
    cbias_ref[...] = -(best + jnp.log2(total)) - math.log2(n_cols)
    pot_ref[...] = (cbias_ref[...] + scale * csq_ref[...]) * (EPS * LN2)
    offset = jnp.max(info_ref[:1, :])
    far = jnp.min(cbias_ref[...]) + offset < HEADROOM_LIMIT
    usable = jnp.logical_and(jnp.min(info_ref[1:, :]) > 0.5, jnp.logical_not(far))

    @pl.when(usable)
    def _():
        gain = jnp.exp2(cbias_ref[...] + (offset + HEADROOM))
        for r in range(0, rows, 128):
            terms_ref, first, place = (low_ref, 0, r) if r < half else (high_ref, 8, r - half)
            total = jnp.zeros((128, 128), jnp.float32)
            for o in range(0, cols, 128):
                total = total + terms_ref[place : place + 128, o : o + 128] * gain[:, o : o + 128]
            value = to_row(jnp.sum(total, axis=1, keepdims=True), 8) * (factor * 2.0 ** (1.0 - HEADROOM) / scale)
            out_ref[first : first + 8, :, place : place + 128] = value

    @pl.when(jnp.logical_not(usable))
    def _():
        def some_rows(r, _):
            own = pl.ds(pl.multiple_of(r * 128, 128), 128)
            xs = x_ref[own, :]
            rbias = jnp.broadcast_to(rbias_ref[:, own], (128, 128)).T

            def some_columns(c, state):
                mass, moment = state
                at = pl.ds(pl.multiple_of(c * 128, 128), 128)
                part = nt_dot(xs, y_ref[at, :])
                plan = jnp.exp2((part * scale + cbias_ref[:, at]) + rbias)
                return mass + plan, moment + plan * (part - csq_ref[:, at])

            state = jnp.zeros((128, 128), jnp.float32), jnp.zeros((128, 128), jnp.float32)
            mass, moment = lax.fori_loop(0, cols // 128, some_columns, state)
            mass = to_row(jnp.sum(mass, axis=1, keepdims=True))
            moment = to_row(jnp.sum(moment, axis=1, keepdims=True))
            value = factor * (rsq_ref[:, own][None] * mass - 2.0 * moment)

            @pl.when(r < half // 128)
            def _():
                out_ref[:8, :, own] = jnp.broadcast_to(value, (8, 1, 128))

            @pl.when(r >= half // 128)
            def _():
                there = pl.ds(pl.multiple_of(r * 128 - half, 128), 128)
                out_ref[8:, :, there] = jnp.broadcast_to(value, (8, 1, 128))

            return 0

        lax.fori_loop(0, rows // 128, some_rows, 0)


def reward_part(parts, x, y, rbias, rsq, csq, low, high, info, scale, factor, n_cols):
    rows, cols = x.shape[0], y.shape[0]
    vmem = pl.BlockSpec(memory_space=pltpu.VMEM)
    return pl.pallas_call(
        functools.partial(reward_kernel, scale, factor, n_cols),
        in_specs=[vmem] * 9,
        out_specs=[vmem] * 2,
        out_shape=[
            jax.ShapeDtypeStruct((16, 1, rows // 2), jnp.float32),
            jax.ShapeDtypeStruct((1, cols), jnp.float32),
        ],
        scratch_shapes=[pltpu.VMEM((1, cols), jnp.float32)],
        compiler_params=pltpu.CompilerParams(vmem_limit_bytes=8 * 2**20),
        cost_estimate=pl.CostEstimate(flops=2 * rows * cols, bytes_accessed=4 * rows * cols, transcendentals=0),
    )(parts, x, y, rbias, rsq, csq, low, high, info)


def copy_kernel(in_ref, out_ref):
    out_ref[...] = jnp.broadcast_to(in_ref[...][None], out_ref.shape)


def copies(a, n):
    return pl.pallas_call(copy_kernel, out_shape=jax.ShapeDtypeStruct((n,) + a.shape, a.dtype))(a)


def swap(a, axis, bit, before):
    size = lax.axis_size(axis)
    other = lax.ppermute(a, axis, [(i, i ^ bit) for i in range(size)])
    low = (lax.axis_index(axis) & bit) == 0
    return jnp.stack([jnp.where(low, a, other), jnp.where(low, other, a)], axis=before)


def ring_gather(a, axes):
    n = math.prod(lax.axis_size(ax) for ax in axes)
    me = lax.axis_index(axes)
    zeros = (0,) * a.ndim

    def shift(v, by):
        return lax.ppermute(v, axes, [(i, (i + by) % n) for i in range(n)])

    def put(v, owner):
        return lax.dynamic_update_slice(out, v[None], (lax.rem(owner + n, n),) + zeros)

    out = jnp.zeros((n,) + a.shape, a.dtype)
    out = put(a, me)
    up = down = a
    for s in range(1, n // 2):
        up, down = shift(up, 1), shift(down, -1)
        out = put(up, me - s)
        out = put(down, me + s)
    return put(shift(up, 1), me - n // 2)


def merge(parts):
    parts = parts[:, 0]
    best = jnp.max(parts, axis=0)
    return best + jnp.log2(jnp.sum(jnp.exp2(parts - best), axis=0))


def body(logged, fresh, warm):
    depth = logged.shape[1]
    first = lax.axis_index("zh") == 0
    n_rows = logged.shape[0] * 256
    n_cols = fresh.shape[0] * 256

    many, logged, first = lax.optimization_barrier((copies(fresh, 16), logged, first))
    y = lax.all_to_all(many, COL_GROUP, 0, 0).reshape(-1, depth)
    x = swap(ring_gather(logged, ("zh", "zl")), "core", 1, 1).reshape(-1, depth)
    rows, cols = x.shape[0], y.shape[0]

    scale = 2.0 * LOG2E / (depth * EPS)
    xw = x.astype(jnp.float32)
    xsq = jnp.sum(xw * xw, axis=1)
    yw = y.astype(jnp.float32)
    ysq = jnp.sum(yw * yw, axis=1)
    warm = jnp.where(first, warm[:cols], warm[cols:])

    bias = warm * (LOG2E / EPS) - ysq * (0.5 * scale)
    part = lse(x, y, bias, scale, 1, 0.0)
    total = merge(lax.all_to_all(part, ROW_GROUP, 0, 0))
    rbias = -total - math.log2(n_rows)
    row_all = (rbias + xsq * (0.5 * scale)) * (EPS * LN2)

    part, low, high, info = column_part(x, y, rbias[None], xsq[None], (0.5 * ysq)[None], scale, 30.0)
    parts = lax.all_to_all(part, COL_GROUP, 0, 0)
    part, col_half = reward_part(
        parts, x, y, rbias[None], xsq[None], (0.5 * ysq)[None], low, high, info, scale, -n_rows / depth, n_cols
    )
    got = lax.all_to_all(part, ROW_GROUP, 0, 0)
    reward = jnp.sum(got[:, 0], axis=0)
    theirs = lax.ppermute(col_half, "zh", [(0, 1), (1, 0)])
    mine, theirs = col_half[0], theirs[0]
    col_potential = jnp.where(first, jnp.concatenate([mine, theirs]), jnp.concatenate([theirs, mine]))
    row_potential = jnp.where(first, row_all[: rows // 2], row_all[rows // 2 :])
    return row_potential, col_potential, reward


def solution(mesh):
    fine = Mesh(mesh.devices.reshape(2, 4, 4, 4, 2), AXES)
    return jax.shard_map(
        body,
        mesh=fine,
        in_specs=(P(AXES, None), P(("zl", "core", "zh", "y", "x"), None), P(("zl", "core"))),
        out_specs=(P(("zh", "y", "x")), P(("zl", "core")), P(("zh", "y", "x"))),
        check_vma=False,
    )
```

profile of v0, /device:TPU:1, one launch (start us, length us, event | category | flops | bytes accessed | tf_op | source)
XLA Modules:
  0.0 411.9 jit_solution(195030507915147668)
XLA Ops:
  0.6 2.5 shard_map.58
  3.1 6.4 %collective-permute-start.1 = (bf16[128,256]{1,0:T(8,128)(2,1)S(1)}, bf16[128,256]{1,0:T(8,128)(2,1)S(1)}, u32[]{:S(2)}, u32[]{:S(2)}) collective-permute-start(bf16[128,256]{1,0:T(8,128)(2,1)S(1)} %copy-done.2), channel_id=1, source_target_pairs={{0,134},{2,0},{4,2},{6,4},{128,6},{130,128},{132,130},{134,132},{1... | collective-permute-start | bytes 196616 | tf_op jit(solution)/shard_map/ppermute | solution.py:300
  9.5 6.8 %all-to-all-start = ((bf16[16,256,256]{2,1,0:T(8,128)(2,1)}), bf16[16,256,256]{2,1,0:T(8,128)(2,1)S(1)}, u32[]{:S(2)}, u32[]{:S(2)}) async-start(bf16[16,256,256]{2,1,0:T(8,128)(2,1)} %shard_map.58), calls=%async_computation | async-start | bytes 4194304 | tf_op jit(solution)/shard_map/all_to_all | solution.py:328
  16.4 2.7 collective-permute-start.3
  19.2 1.3 collective-permute-done.3
  20.5 3.0 collective-permute-start.5
  23.5 0.3 collective-permute-done.2
  23.8 4.6 %collective-permute-done.4 = bf16[128,256]{1,0:T(8,128)(2,1)S(1)} collective-permute-done((bf16[128,256]{1,0:T(8,128)(2,1)S(1)}, bf16[128,256]{1,0:T(8,128)(2,1)S(1)}, u32[]{:S(2)}, u32[]{:S(2)}) %collective-permute-start.4) | collective-permute-done | bytes 65568 | tf_op jit(solution)/shard_map/ppermute | solution.py:300
  28.5 4.6 %collective-permute-done.6 = bf16[128,256]{1,0:T(8,128)(2,1)S(1)} collective-permute-done((bf16[128,256]{1,0:T(8,128)(2,1)S(1)}, bf16[128,256]{1,0:T(8,128)(2,1)S(1)}, u32[]{:S(2)}, u32[]{:S(2)}) %collective-permute-start.6) | collective-permute-done | bytes 65568 | tf_op jit(solution)/shard_map/ppermute | solution.py:300
  33.1 4.6 %collective-permute-start.7 = (bf16[8,128,256]{2,1,0:T(8,128)(2,1)S(1)}, bf16[8,128,256]{2,1,0:T(8,128)(2,1)S(1)}, u32[]{:S(2)}, u32[]{:S(2)}) collective-permute-start(bf16[8,128,256]{2,1,0:T(8,128)(2,1)S(1)} %bitcast_dynamic-update-slice_fusion), channel_id=1, source_target_pairs={{0,1},{1,0},{2,3},{3,2},{4,5},{5,4},{6,7},{7,6},{8,9},{9,8},{10,11... | collective-permute-start | bytes 1572872 | tf_op jit(solution)/shard_map/ppermute | solution.py:289
  37.7 1.5 collective-permute-done.7
  39.3 0.8 copy-done
  40.1 0.2 copy-done.1
  40.3 0.1 pad_maximum_fusion
  40.4 5.6 %all-to-all-done = bf16[16,256,256]{2,1,0:T(8,128)(2,1)S(1)} async-done(((bf16[16,256,256]{2,1,0:T(8,128)(2,1)}), bf16[16,256,256]{2,1,0:T(8,128)(2,1)S(1)}, u32[]{:S(2)}, u32[]{:S(2)}) %all-to-all-start) | async-done | bytes 2097184 | tf_op jit(solution)/shard_map/all_to_all | solution.py:328
  46.0 0.6 multiply_reduce_fusion
  46.7 0.1 reshape.93.few_ref
  46.8 7.2 %shard_map.59 = f32[16,1,2048]{2,1,0:T(1,128)} custom-call(bf16[2048,256]{1,0:T(8,128)(2,1)S(1)} %bitcast.48, bf16[4096,256]{1,0:T(8,128)(2,1)S(1)} %bitcast.45, f32[1,4096]{1,0:T(1,128)S(1)} %bitcast.57, f32[1,256]{1,0:T(1,128)S(1)} %reshape.93.few_ref), custom_call_target="tpu_custom_call" | custom-call | flops 4294967296 | bytes 3145728 | tf_op jit(solution)/shard_map/pallas_call | solution.py:89
  54.0 107.0 %all-to-all-start.1 = ((f32[16,1,2048]{2,1,0:T(1,128)}), f32[16,1,2048]{2,1,0:T(1,128)S(1)}, u32[]{:S(2)}, u32[]{:S(2)}) async-start(f32[16,1,2048]{2,1,0:T(1,128)} %shard_map.59), calls=%async_computation.1 | async-start | bytes 262144 | tf_op jit(solution)/shard_map/all_to_all | solution.py:341
  161.0 1.6 multiply_reduce_fusion.1
  162.6 7.6 %all-to-all-done.1 = f32[16,1,2048]{2,1,0:T(1,128)S(1)} async-done(((f32[16,1,2048]{2,1,0:T(1,128)}), f32[16,1,2048]{2,1,0:T(1,128)S(1)}, u32[]{:S(2)}, u32[]{:S(2)}) %all-to-all-start.1) | async-done | bytes 131104 | tf_op jit(solution)/shard_map/all_to_all | solution.py:341
  170.1 0.1 reduce_max.9
  170.2 0.1 fusion.2
  170.3 114.6 %shard_map.60 = (f32[16,1,4096]{2,1,0:T(1,128)S(1)}, f32[1024,4096]{1,0:T(8,128)S(1)}, f32[1024,4096]{1,0:T(8,128)S(1)}, f32[2,128]{1,0:T(2,128)S(1)}) custom-call(bf16[2048,256]{1,0:T(8,128)(2,1)S(1)} %bitcast.49, bf16[4096,256]{1,0:T(8,128)(2,1)S(1)} %bitcast.46, f32[1,2048]{1,0:T(1,128)S(1)} %bitcast.55, f32[1,2048]{1,0:T(1,128)S(1)} %bitcast.51, ...), custom_call_target="tpu_custom_call" | custom-call | flops 4294967296 | bytes 3145728 | tf_op jit(solution)/shard_map/pallas_call | solution.py:186
  284.9 11.7 %all_to_all.20.parts_ref = f32[16,1,4096]{2,1,0:T(1,128)S(1)} all-to-all(f32[16,1,4096]{2,1,0:T(1,128)S(1)} %get-tuple-element.15), channel_id=1, replica_groups=mesh['zh'=2,'y'=4,'x'=4,'zl'=4,'core'=2] {'y','x'}, dimensions={0} | all-to-all | bytes 524288 | tf_op jit(solution)/shard_map/all_to_all | solution.py:346
  296.6 102.3 %shard_map.61 = (f32[16,1,1024]{2,1,0:T(1,128)}, f32[1,4096]{1,0:T(1,128)S(1)}) custom-call(f32[16,1,4096]{2,1,0:T(1,128)S(1)} %all_to_all.20.parts_ref, bf16[2048,256]{1,0:T(8,128)(2,1)S(1)} %bitcast.50, bf16[4096,256]{1,0:T(8,128)(2,1)S(1)} %bitcast.47, f32[1,2048]{1,0:T(1,128)S(1)} %bitcast.56, f32[1,2048]{1,0:T(1,128)S(1)} %bitcast.52, ...), custom_call_target="tpu_custom_call" | custom-call | flops 16777216 | bytes 33554432 | tf_op jit(solution)/shard_map/pallas_call | solution.py:265
  398.9 3.8 all-to-all-start.3
  402.7 5.3 %collective-permute-start.8 = (f32[1,4096]{1,0:T(1,128)S(1)}, f32[1,4096]{1,0:T(1,128)S(1)}, u32[]{:S(2)}, u32[]{:S(2)}) collective-permute-start(f32[1,4096]{1,0:T(1,128)S(1)} %get-tuple-element.19), channel_id=1, source_target_pairs={{0,128},{128,0},{1,129},{129,1},{2,130},{130,2},{3,131},{131,3},{4... | collective-permute-start | bytes 49160 | tf_op jit(solution)/shard_map/ppermute | solution.py:352
  408.1 0.6 slice_select_fusion
  408.6 2.0 collective-permute-done.8
  410.7 0.6 maximum_select_fusion
  411.3 0.6 reduce_sum.39
  (32 shorter events, 0.3 us)
Async XLA Ops:
  0.6 2.5 copy-start.2
  3.1 13.3 %collective-permute-start.1 = (bf16[128,256]{1,0:T(8,128)(2,1)S(1)}, bf16[128,256]{1,0:T(8,128)(2,1)S(1)}, u32[]{:S(2)}, u32[]{:S(2)}) collective-permute-start(bf16[128,256]{1,0:T(8,128)(2,1)S(1)} %copy-done.2), channel_id=1, source_target_pairs={{0,134},{2,0},{4,2},{6,4},{128,6},{130,128},{132,130},{134,132},{1... | collective-permute-start | bytes 196616 | tf_op jit(solution)/shard_map/ppermute | solution.py:300
  9.5 9.7 %collective-permute-start = (bf16[128,256]{1,0:T(8,128)(2,1)S(1)}, bf16[128,256]{1,0:T(8,128)(2,1)S(1)}, u32[]{:S(2)}, u32[]{:S(2)}) collective-permute-start(bf16[128,256]{1,0:T(8,128)(2,1)S(1)} %copy-done.2), channel_id=1, source_target_pairs={{0,2},{2,4},{4,6},{6,128},{128,130},{130,132},{132,134},{134,0},{1... | collective-permute-start | bytes 196616 | tf_op jit(solution)/shard_map/ppermute | solution.py:300
  9.5 36.5 %all-to-all-start = ((bf16[16,256,256]{2,1,0:T(8,128)(2,1)}), bf16[16,256,256]{2,1,0:T(8,128)(2,1)S(1)}, u32[]{:S(2)}, u32[]{:S(2)}) async-start(bf16[16,256,256]{2,1,0:T(8,128)(2,1)} %shard_map.58), calls=%async_computation | async-start | bytes 4194304 | tf_op jit(solution)/shard_map/all_to_all | solution.py:328
  16.4 4.1 collective-permute-start.3
  19.2 4.6 %collective-permute-start.2 = (bf16[128,256]{1,0:T(8,128)(2,1)S(1)}, bf16[128,256]{1,0:T(8,128)(2,1)S(1)}, u32[]{:S(2)}, u32[]{:S(2)}) collective-permute-start(bf16[128,256]{1,0:T(8,128)(2,1)S(1)} %collective-permute-done), channel_id=1, source_target_pairs={{0,2},{2,4},{4,6},{6,128},{128,130},{130,132},{132,134},{134,0},{1... | collective-permute-start | bytes 196616 | tf_op jit(solution)/shard_map/ppermute | solution.py:300
  20.5 7.9 %collective-permute-start.5 = (bf16[128,256]{1,0:T(8,128)(2,1)S(1)}, bf16[128,256]{1,0:T(8,128)(2,1)S(1)}, u32[]{:S(2)}, u32[]{:S(2)}) collective-permute-start(bf16[128,256]{1,0:T(8,128)(2,1)S(1)} %collective-permute-done.3), channel_id=1, source_target_pairs={{0,134},{2,0},{4,2},{6,4},{128,6},{130,128},{132,130},{134,132},{1... | collective-permute-start | bytes 196616 | tf_op jit(solution)/shard_map/ppermute | solution.py:300
  23.8 4.6 %collective-permute-start.4 = (bf16[128,256]{1,0:T(8,128)(2,1)S(1)}, bf16[128,256]{1,0:T(8,128)(2,1)S(1)}, u32[]{:S(2)}, u32[]{:S(2)}) collective-permute-start(bf16[128,256]{1,0:T(8,128)(2,1)S(1)} %collective-permute-done.2), channel_id=1, source_target_pairs={{0,2},{2,4},{4,6},{6,128},{128,130},{130,132},{132,134},{134,0},{1... | collective-permute-start | bytes 196616 | tf_op jit(solution)/shard_map/ppermute | solution.py:300
  28.4 4.6 %collective-permute-start.6 = (bf16[128,256]{1,0:T(8,128)(2,1)S(1)}, bf16[128,256]{1,0:T(8,128)(2,1)S(1)}, u32[]{:S(2)}, u32[]{:S(2)}) collective-permute-start(bf16[128,256]{1,0:T(8,128)(2,1)S(1)} %collective-permute-done.4), channel_id=1, source_target_pairs={{0,2},{2,4},{4,6},{6,128},{128,130},{130,132},{132,134},{134,0},{1... | collective-permute-start | bytes 196616 | tf_op jit(solution)/shard_map/ppermute | solution.py:300
  33.1 6.2 %collective-permute-start.7 = (bf16[8,128,256]{2,1,0:T(8,128)(2,1)S(1)}, bf16[8,128,256]{2,1,0:T(8,128)(2,1)S(1)}, u32[]{:S(2)}, u32[]{:S(2)}) collective-permute-start(bf16[8,128,256]{2,1,0:T(8,128)(2,1)S(1)} %bitcast_dynamic-update-slice_fusion), channel_id=1, source_target_pairs={{0,1},{1,0},{2,3},{3,2},{4,5},{5,4},{6,7},{7,6},{8,9},{9,8},{10,11... | collective-permute-start | bytes 1572872 | tf_op jit(solution)/shard_map/ppermute | solution.py:289
  39.3 0.8 copy-start
  39.3 1.0 copy-start.1
  40.3 6.3 %copy-start.3 = (f32[8192]{0:T(1024)S(1)}, f32[8192]{0:T(1024)}, u32[]{:S(2)}) copy-start(f32[8192]{0:T(1024)} %param.5) | copy-start | bytes 98308
  54.0 116.2 %all-to-all-start.1 = ((f32[16,1,2048]{2,1,0:T(1,128)}), f32[16,1,2048]{2,1,0:T(1,128)S(1)}, u32[]{:S(2)}, u32[]{:S(2)}) async-start(f32[16,1,2048]{2,1,0:T(1,128)} %shard_map.59), calls=%async_computation.1 | async-start | bytes 262144 | tf_op jit(solution)/shard_map/all_to_all | solution.py:341
  398.9 12.4 %all-to-all-start.3 = ((f32[16,1,1024]{2,1,0:T(1,128)}), f32[16,1,1024]{2,1,0:T(1,128)S(1)}, u32[]{:S(2)}, u32[]{:S(2)}) async-start(f32[16,1,1024]{2,1,0:T(1,128)} %get-tuple-element.20), calls=%async_computation.3 | async-start | bytes 131072 | tf_op jit(solution)/shard_map/all_to_all | solution.py:350
  402.7 7.9 %collective-permute-start.8 = (f32[1,4096]{1,0:T(1,128)S(1)}, f32[1,4096]{1,0:T(1,128)S(1)}, u32[]{:S(2)}, u32[]{:S(2)}) collective-permute-start(f32[1,4096]{1,0:T(1,128)S(1)} %get-tuple-element.19), channel_id=1, source_target_pairs={{0,128},{128,0},{1,129},{129,1},{2,130},{130,2},{3,131},{131,3},{4... | collective-permute-start | bytes 49160 | tf_op jit(solution)/shard_map/ppermute | solution.py:352
where the time goes:
time: 411 us; the launch traced here: 412 us
  Pallas kernels  227 us (55%)
  starting transfers between devices  140 us (34%)
  waiting for transfers between devices  27.4 us (7%)
  blocking collectives  11.7 us (3%)
  other arithmetic  4.4 us (1%)
    pallas_call x1, Pallas kernels, column_part(): pl.pallas_call(functools.partial(column_kernel, scale, raised), in_specs=...  115 us
    all_to_all x1, starting transfers between devices, body(): total = merge(lax.all_to_all(part, ROW_GROUP, 0, 0))  107 us
    pallas_call x1, Pallas kernels, reward_part(): pl.pallas_call(functools.partial(reward_kernel, scale, factor, n_cols), i...  102 us
    ppermute x7, starting transfers between devices, shift(): return lax.ppermute(v, axes, [(i, (i + by) % n) for i in range(n)])  12.2 us
    all_to_all x1, blocking collectives, body(): parts = lax.all_to_all(part, COL_GROUP, 0, 0)  11.7 us
    ppermute x7, waiting for transfers between devices, shift(): return lax.ppermute(v, axes, [(i, (i + by) % n) for i in range(n)])  10.8 us
  transfers between devices with their start and end apart: 12, of which 8 were waited for; matrix products, arithmetic and copies ran while one was open for 1% of the time, Pallas kernels for 0%

commit v1 on v0

--- a/solution.py
+++ b/solution.py
@@ -11,8 +11,8 @@
 
 EPS = 0.01
 AXES = ("zh", "y", "x", "zl", "core")
-ROW_GROUP = ("zh", "zl", "core")
-COL_GROUP = ("y", "x")
+ROW_GROUP = ("zh", "core", "zl")
+COL_GROUP = ("x", "y")
 LN2 = math.log(2.0)
 LOG2E = 1.0 / LN2
 
@@ -209,7 +209,11 @@
     best = functools.reduce(jnp.maximum, [parts_ref[i] for i in range(parts_ref.shape[0])])
     total = functools.reduce(jnp.add, [jnp.exp2(parts_ref[i] - best) for i in range(parts_ref.shape[0])])
     cbias_ref[...] = -(best + jnp.log2(total)) - math.log2(n_cols)
-    pot_ref[...] = (cbias_ref[...] + scale * csq_ref[...]) * (EPS * LN2)
+    potential = (cbias_ref[...] + scale * csq_ref[...]) * (EPS * LN2)
+    size = cols // 16
+    for b in range(16):
+        place = (b % 4 * 4 + b // 4) * size
+        pot_ref[:, place : place + size] = potential[:, b * size : (b + 1) * size]
     offset = jnp.max(info_ref[:1, :])
     far = jnp.min(cbias_ref[...]) + offset < HEADROOM_LIMIT
     usable = jnp.logical_and(jnp.min(info_ref[1:, :]) > 0.5, jnp.logical_not(far))
@@ -334,7 +338,7 @@
     xsq = jnp.sum(xw * xw, axis=1)
     yw = y.astype(jnp.float32)
     ysq = jnp.sum(yw * yw, axis=1)
-    warm = jnp.where(first, warm[:cols], warm[cols:])
+    warm = jnp.where(first, warm[:cols], warm[cols:]).reshape(4, 4, -1).transpose(1, 0, 2).reshape(-1)
 
     bias = warm * (LOG2E / EPS) - ysq * (0.5 * scale)
     part = lse(x, y, bias, scale, 1, 0.0)

time: 411 us -> 409 us (level)
  waiting for transfers between devices: 27.4 us -> 22.6 us
where the time goes in v1:
time: 409 us; the launch traced here: 408 us
  Pallas kernels  224 us (55%)
  starting transfers between devices  144 us (35%)
  waiting for transfers between devices  22.6 us (6%)
  blocking collectives  11.1 us (3%)
  other arithmetic  4.42 us (1%)
    pallas_call x1, Pallas kernels, column_part(): pl.pallas_call(functools.partial(column_kernel, scale, raised), in_specs=...  115 us
    all_to_all x1, starting transfers between devices, body(): total = merge(lax.all_to_all(part, ROW_GROUP, 0, 0))  110 us
    pallas_call x1, Pallas kernels, reward_part(): pl.pallas_call(functools.partial(reward_kernel, scale, factor, n_cols), i...  100 us
    ppermute x7, starting transfers between devices, shift(): return lax.ppermute(v, axes, [(i, (i + by) % n) for i in range(n)])  12.2 us
    all_to_all x1, blocking collectives, body(): parts = lax.all_to_all(part, COL_GROUP, 0, 0)  11.1 us
    ppermute x7, waiting for transfers between devices, shift(): return lax.ppermute(v, axes, [(i, (i + by) % n) for i in range(n)])  10.8 us
  transfers between devices with their start and end apart: 12, of which 8 were waited for; matrix products, arithmetic and copies ran while one was open for 1% of the time, Pallas kernels for 0%

profile of v1, /device:TPU:1, one launch (start us, length us, event | category | flops | bytes accessed | tf_op | source)
XLA Modules:
  0.0 408.4 jit_solution(10534278396031423733)
XLA Ops:
  0.6 2.5 shard_map.58
  3.1 6.4 %collective-permute-start.1 = (bf16[128,256]{1,0:T(8,128)(2,1)S(1)}, bf16[128,256]{1,0:T(8,128)(2,1)S(1)}, u32[]{:S(2)}, u32[]{:S(2)}) collective-permute-start(bf16[128,256]{1,0:T(8,128)(2,1)S(1)} %copy-done.2), channel_id=1, source_target_pairs={{0,134},{2,0},{4,2},{6,4},{128,6},{130,128},{132,130},{134,132},{1... | collective-permute-start | bytes 196616 | tf_op jit(solution)/shard_map/ppermute | solution.py:304
  9.5 6.8 %all-to-all-start = ((bf16[16,256,256]{2,1,0:T(8,128)(2,1)}), bf16[16,256,256]{2,1,0:T(8,128)(2,1)S(1)}, u32[]{:S(2)}, u32[]{:S(2)}) async-start(bf16[16,256,256]{2,1,0:T(8,128)(2,1)} %shard_map.58), calls=%async_computation | async-start | bytes 4194304 | tf_op jit(solution)/shard_map/all_to_all | solution.py:332
  16.4 2.7 collective-permute-start.3
  19.2 1.3 collective-permute-done.3
  20.5 3.0 collective-permute-start.5
  23.5 0.3 collective-permute-done.2
  23.8 4.6 %collective-permute-done.4 = bf16[128,256]{1,0:T(8,128)(2,1)S(1)} collective-permute-done((bf16[128,256]{1,0:T(8,128)(2,1)S(1)}, bf16[128,256]{1,0:T(8,128)(2,1)S(1)}, u32[]{:S(2)}, u32[]{:S(2)}) %collective-permute-start.4) | collective-permute-done | bytes 65568 | tf_op jit(solution)/shard_map/ppermute | solution.py:304
  28.5 4.6 %collective-permute-done.6 = bf16[128,256]{1,0:T(8,128)(2,1)S(1)} collective-permute-done((bf16[128,256]{1,0:T(8,128)(2,1)S(1)}, bf16[128,256]{1,0:T(8,128)(2,1)S(1)}, u32[]{:S(2)}, u32[]{:S(2)}) %collective-permute-start.6) | collective-permute-done | bytes 65568 | tf_op jit(solution)/shard_map/ppermute | solution.py:304
  33.1 4.6 %collective-permute-start.7 = (bf16[8,128,256]{2,1,0:T(8,128)(2,1)S(1)}, bf16[8,128,256]{2,1,0:T(8,128)(2,1)S(1)}, u32[]{:S(2)}, u32[]{:S(2)}) collective-permute-start(bf16[8,128,256]{2,1,0:T(8,128)(2,1)S(1)} %bitcast_dynamic-update-slice_fusion), channel_id=1, source_target_pairs={{0,1},{1,0},{2,3},{3,2},{4,5},{5,4},{6,7},{7,6},{8,9},{9,8},{10,11... | collective-permute-start | bytes 1572872 | tf_op jit(solution)/shard_map/ppermute | solution.py:293
  37.8 1.4 collective-permute-done.7
  39.3 0.8 copy-done
  40.1 0.2 copy-done.1
  40.3 0.1 pad_maximum_fusion
  40.4 2.0 all-to-all-done
  42.4 0.6 multiply_reduce_fusion
  43.1 0.1 reshape.123.few_ref
  43.2 7.2 %shard_map.59 = f32[16,1,2048]{2,1,0:T(1,128)} custom-call(bf16[2048,256]{1,0:T(8,128)(2,1)S(1)} %bitcast.49, bf16[4096,256]{1,0:T(8,128)(2,1)S(1)} %bitcast.46, f32[1,4096]{1,0:T(1,128)S(1)} %sub.31.bias_ref, f32[1,256]{1,0:T(1,128)S(1)} %reshape.123.few_ref), custom_call_target="tpu_custom_call" | custom-call | flops 4294967296 | bytes 3145728 | tf_op jit(solution)/shard_map/pallas_call | solution.py:89
  50.4 109.7 %all-to-all-start.1 = ((f32[16,1,2048]{2,1,0:T(1,128)}), f32[16,1,2048]{2,1,0:T(1,128)S(1)}, u32[]{:S(2)}, u32[]{:S(2)}) async-start(f32[16,1,2048]{2,1,0:T(1,128)} %shard_map.59), calls=%async_computation.1 | async-start | bytes 262144 | tf_op jit(solution)/shard_map/all_to_all | solution.py:345
  160.1 1.6 multiply_reduce_fusion.1
  161.7 6.4 %all-to-all-done.1 = f32[16,1,2048]{2,1,0:T(1,128)S(1)} async-done(((f32[16,1,2048]{2,1,0:T(1,128)}), f32[16,1,2048]{2,1,0:T(1,128)S(1)}, u32[]{:S(2)}, u32[]{:S(2)}) %all-to-all-start.1) | async-done | bytes 131104 | tf_op jit(solution)/shard_map/all_to_all | solution.py:345
  168.1 0.1 reduce_max.9
  168.2 0.1 fusion.2
  168.3 114.6 %shard_map.60 = (f32[16,1,4096]{2,1,0:T(1,128)S(1)}, f32[1024,4096]{1,0:T(8,128)S(1)}, f32[1024,4096]{1,0:T(8,128)S(1)}, f32[2,128]{1,0:T(2,128)S(1)}) custom-call(bf16[2048,256]{1,0:T(8,128)(2,1)S(1)} %bitcast.50, bf16[4096,256]{1,0:T(8,128)(2,1)S(1)} %bitcast.47, f32[1,2048]{1,0:T(1,128)S(1)} %bitcast.56, f32[1,2048]{1,0:T(1,128)S(1)} %bitcast.52, ...), custom_call_target="tpu_custom_call" | custom-call | flops 4294967296 | bytes 3145728 | tf_op jit(solution)/shard_map/pallas_call | solution.py:186
  282.9 11.1 %all_to_all.20.parts_ref = f32[16,1,4096]{2,1,0:T(1,128)S(1)} all-to-all(f32[16,1,4096]{2,1,0:T(1,128)S(1)} %get-tuple-element.15), channel_id=1, replica_groups=mesh['zh'=2,'y'=4,'x'=4,'zl'=4,'core'=2] {'x','y'}, dimensions={0} | all-to-all | bytes 524288 | tf_op jit(solution)/shard_map/all_to_all | solution.py:350
  294.0 100.1 %shard_map.61 = (f32[16,1,1024]{2,1,0:T(1,128)}, f32[1,4096]{1,0:T(1,128)S(1)}) custom-call(f32[16,1,4096]{2,1,0:T(1,128)S(1)} %all_to_all.20.parts_ref, bf16[2048,256]{1,0:T(8,128)(2,1)S(1)} %bitcast.51, bf16[4096,256]{1,0:T(8,128)(2,1)S(1)} %bitcast.48, f32[1,2048]{1,0:T(1,128)S(1)} %bitcast.57, f32[1,2048]{1,0:T(1,128)S(1)} %bitcast.53, ...), custom_call_target="tpu_custom_call" | custom-call | flops 16777216 | bytes 33554432 | tf_op jit(solution)/shard_map/pallas_call | solution.py:269
  394.1 5.1 %all-to-all-start.3 = ((f32[16,1,1024]{2,1,0:T(1,128)}), f32[16,1,1024]{2,1,0:T(1,128)S(1)}, u32[]{:S(2)}, u32[]{:S(2)}) async-start(f32[16,1,1024]{2,1,0:T(1,128)} %get-tuple-element.20), calls=%async_computation.3 | async-start | bytes 131072 | tf_op jit(solution)/shard_map/all_to_all | solution.py:354
  399.2 5.3 %collective-permute-start.8 = (f32[1,4096]{1,0:T(1,128)S(1)}, f32[1,4096]{1,0:T(1,128)S(1)}, u32[]{:S(2)}, u32[]{:S(2)}) collective-permute-start(f32[1,4096]{1,0:T(1,128)S(1)} %get-tuple-element.19), channel_id=1, source_target_pairs={{0,128},{128,0},{1,129},{129,1},{2,130},{130,2},{3,131},{131,3},{4... | collective-permute-start | bytes 49160 | tf_op jit(solution)/shard_map/ppermute | solution.py:356
  404.6 0.6 slice_select_fusion
  405.2 2.0 collective-permute-done.8
  407.1 0.6 maximum_select_fusion
  407.8 0.6 reduce_sum.39
  (36 shorter events, 0.4 us)
Async XLA Ops:
  0.6 2.5 copy-start.2
  3.1 34.6 %copy-start.3 = (f32[8192]{0:T(1024)S(1)}, f32[8192]{0:T(1024)}, u32[]{:S(2)}) copy-start(f32[8192]{0:T(1024)} %param.5) | copy-start | bytes 98308
  3.1 13.3 %collective-permute-start.1 = (bf16[128,256]{1,0:T(8,128)(2,1)S(1)}, bf16[128,256]{1,0:T(8,128)(2,1)S(1)}, u32[]{:S(2)}, u32[]{:S(2)}) collective-permute-start(bf16[128,256]{1,0:T(8,128)(2,1)S(1)} %copy-done.2), channel_id=1, source_target_pairs={{0,134},{2,0},{4,2},{6,4},{128,6},{130,128},{132,130},{134,132},{1... | collective-permute-start | bytes 196616 | tf_op jit(solution)/shard_map/ppermute | solution.py:304
  9.5 9.7 %collective-permute-start = (bf16[128,256]{1,0:T(8,128)(2,1)S(1)}, bf16[128,256]{1,0:T(8,128)(2,1)S(1)}, u32[]{:S(2)}, u32[]{:S(2)}) collective-permute-start(bf16[128,256]{1,0:T(8,128)(2,1)S(1)} %copy-done.2), channel_id=1, source_target_pairs={{0,2},{2,4},{4,6},{6,128},{128,130},{130,132},{132,134},{134,0},{1... | collective-permute-start | bytes 196616 | tf_op jit(solution)/shard_map/ppermute | solution.py:304
  9.5 32.9 %all-to-all-start = ((bf16[16,256,256]{2,1,0:T(8,128)(2,1)}), bf16[16,256,256]{2,1,0:T(8,128)(2,1)S(1)}, u32[]{:S(2)}, u32[]{:S(2)}) async-start(bf16[16,256,256]{2,1,0:T(8,128)(2,1)} %shard_map.58), calls=%async_computation | async-start | bytes 4194304 | tf_op jit(solution)/shard_map/all_to_all | solution.py:332
  16.4 4.1 collective-permute-start.3
  19.2 4.6 %collective-permute-start.2 = (bf16[128,256]{1,0:T(8,128)(2,1)S(1)}, bf16[128,256]{1,0:T(8,128)(2,1)S(1)}, u32[]{:S(2)}, u32[]{:S(2)}) collective-permute-start(bf16[128,256]{1,0:T(8,128)(2,1)S(1)} %collective-permute-done), channel_id=1, source_target_pairs={{0,2},{2,4},{4,6},{6,128},{128,130},{130,132},{132,134},{134,0},{1... | collective-permute-start | bytes 196616 | tf_op jit(solution)/shard_map/ppermute | solution.py:304
  20.5 7.9 %collective-permute-start.5 = (bf16[128,256]{1,0:T(8,128)(2,1)S(1)}, bf16[128,256]{1,0:T(8,128)(2,1)S(1)}, u32[]{:S(2)}, u32[]{:S(2)}) collective-permute-start(bf16[128,256]{1,0:T(8,128)(2,1)S(1)} %collective-permute-done.3), channel_id=1, source_target_pairs={{0,134},{2,0},{4,2},{6,4},{128,6},{130,128},{132,130},{134,132},{1... | collective-permute-start | bytes 196616 | tf_op jit(solution)/shard_map/ppermute | solution.py:304
  23.8 4.6 %collective-permute-start.4 = (bf16[128,256]{1,0:T(8,128)(2,1)S(1)}, bf16[128,256]{1,0:T(8,128)(2,1)S(1)}, u32[]{:S(2)}, u32[]{:S(2)}) collective-permute-start(bf16[128,256]{1,0:T(8,128)(2,1)S(1)} %collective-permute-done.2), channel_id=1, source_target_pairs={{0,2},{2,4},{4,6},{6,128},{128,130},{130,132},{132,134},{134,0},{1... | collective-permute-start | bytes 196616 | tf_op jit(solution)/shard_map/ppermute | solution.py:304
  28.4 4.6 %collective-permute-start.6 = (bf16[128,256]{1,0:T(8,128)(2,1)S(1)}, bf16[128,256]{1,0:T(8,128)(2,1)S(1)}, u32[]{:S(2)}, u32[]{:S(2)}) collective-permute-start(bf16[128,256]{1,0:T(8,128)(2,1)S(1)} %collective-permute-done.4), channel_id=1, source_target_pairs={{0,2},{2,4},{4,6},{6,128},{128,130},{130,132},{132,134},{134,0},{1... | collective-permute-start | bytes 196616 | tf_op jit(solution)/shard_map/ppermute | solution.py:304
  33.1 6.2 %collective-permute-start.7 = (bf16[8,128,256]{2,1,0:T(8,128)(2,1)S(1)}, bf16[8,128,256]{2,1,0:T(8,128)(2,1)S(1)}, u32[]{:S(2)}, u32[]{:S(2)}) collective-permute-start(bf16[8,128,256]{2,1,0:T(8,128)(2,1)S(1)} %bitcast_dynamic-update-slice_fusion), channel_id=1, source_target_pairs={{0,1},{1,0},{2,3},{3,2},{4,5},{5,4},{6,7},{7,6},{8,9},{9,8},{10,11... | collective-permute-start | bytes 1572872 | tf_op jit(solution)/shard_map/ppermute | solution.py:293
  39.3 0.8 copy-start
  39.3 1.0 copy-start.1
  50.4 117.8 %all-to-all-start.1 = ((f32[16,1,2048]{2,1,0:T(1,128)}), f32[16,1,2048]{2,1,0:T(1,128)S(1)}, u32[]{:S(2)}, u32[]{:S(2)}) async-start(f32[16,1,2048]{2,1,0:T(1,128)} %shard_map.59), calls=%async_computation.1 | async-start | bytes 262144 | tf_op jit(solution)/shard_map/all_to_all | solution.py:345
  394.1 13.7 %all-to-all-start.3 = ((f32[16,1,1024]{2,1,0:T(1,128)}), f32[16,1,1024]{2,1,0:T(1,128)S(1)}, u32[]{:S(2)}, u32[]{:S(2)}) async-start(f32[16,1,1024]{2,1,0:T(1,128)} %get-tuple-element.20), calls=%async_computation.3 | async-start | bytes 131072 | tf_op jit(solution)/shard_map/all_to_all | solution.py:354
  399.2 7.9 %collective-permute-start.8 = (f32[1,4096]{1,0:T(1,128)S(1)}, f32[1,4096]{1,0:T(1,128)S(1)}, u32[]{:S(2)}, u32[]{:S(2)}) collective-permute-start(f32[1,4096]{1,0:T(1,128)S(1)} %get-tuple-element.19), channel_id=1, source_target_pairs={{0,128},{128,0},{1,129},{129,1},{2,130},{130,2},{3,131},{131,3},{4... | collective-permute-start | bytes 49160 | tf_op jit(solution)/shard_map/ppermute | solution.py:356
